TPU v7x, 32 devices: a whole 2x2x4 slice. The times are simulated.
32 devices in a mesh: band: 4 (over z), owner: 8 (over y, x, core).
Axes of the slice: x: 2, y: 2, z: 4, core: 2. Of those that a mesh axis runs over, the one named last changes fastest.
Arguments:
- user_factors: float32 [16384, 256], P(('band', 'owner')), may hold values from -1.5 to 1.5
- item_factors: float32 [4096, 256], P(('band', 'owner')), may hold values from -1.5 to 1.5
- ratings: bfloat16 [3, 512, 128, 128], P(None, ('band', 'owner')), may hold values from -6 to 6
- tile_users: int32 [3, 512], P(None, ('band', 'owner')), may hold values from 0 to 3, as said below
- tile_items: int32 [3, 512], P(None, ('band', 'owner')), may hold values from 0 to 7, as said below
- tile_count: int32 [3, 32], P(None, ('band', 'owner')), may hold values from 1 to 16, as said below
Outputs:
- user_out: float32 [16384, 256], P(('band', 'owner'))
- item_out: float32 [4096, 256], P(('band', 'owner'))
Inputs may be any that keep to these rules, and one draw needn't show every extreme that they name: `tile_users`: within one device and tick, the slots name distinct tiles (user row, item column). `tile_items`: paired with tile_users: the slots of one device and tick name distinct tiles. `tile_count`: each value is 16, 8 or 4, at least 1; in every tick some device has 16.
All inputs are finite; a program needn't handle non-finite values.
Results may differ from a plain program's by a relative error of at most 0.0003.
Values sent between devices are 32-bit elements; how exact they have to be, the bound alone decides.
A program may use at most 64 MiB of HBM per device.

v0:
```python
import jax
import jax.numpy as jnp
from jax import lax
from jax.sharding import PartitionSpec as P

R = 256
P_SIZE = 1024
TILE = 128
TICKS = 3
K_MAX = 16


user_rate = 0.02
item_rate = 0.005
shrink_rate = 0.05
highest = lax.Precision.HIGHEST


def passed_along(block, axis, distance):
    devices = range(lax.axis_size(axis))
    route = [((i - distance) % len(devices), i) for i in devices]
    return lax.ppermute(block, axis, route)


def dense_step(user_block, item_shard, rating_tiles, tile_rows, tile_cols, filled):
    tile_rows_count = user_block.shape[0]
    user_flat = user_block.reshape(-1, R)
    active = (jnp.arange(K_MAX) < filled).astype(jnp.float32)
    user_hot = (tile_rows[:, None] == jnp.arange(tile_rows_count)[None, :]).astype(
        jnp.float32
    ) * active[:, None]
    item_hot = (tile_cols[:, None] == jnp.arange(P_SIZE // TILE)[None, :]).astype(jnp.float32)
    rating_dense = jnp.einsum(
        "kt,ks,kui->tusi", user_hot, item_hot, rating_tiles.astype(jnp.float32), precision=highest
    ).reshape(tile_rows_count * TILE, P_SIZE)
    cell_mask = jnp.einsum("kt,ks->ts", user_hot, item_hot, precision=highest)
    mask_dense = jnp.broadcast_to(
        cell_mask[:, None, :, None], (tile_rows_count, TILE, P_SIZE // TILE, TILE)
    ).reshape(tile_rows_count * TILE, P_SIZE)
    piece = lax.all_gather(item_shard, "owner", axis=0, tiled=True)
    predicted = jnp.dot(user_flat, piece.T, precision=highest)
    errors = (rating_dense - predicted) * mask_dense
    user_grad = jnp.dot(errors, piece, precision=highest)
    item_rows = jnp.dot(errors.T, user_flat, precision=highest)
    item_grad = item_rows
    user_grad, item_grad = (user_grad, item_grad)
    return (user_grad.reshape(user_block.shape), item_grad)


def shards(user_factors, item_factors, ratings, tile_users, tile_items, tile_count):
    user_block = user_factors.reshape(-1, TILE, R)
    item_shard = item_factors
    for tick_index in range(TICKS):
        user_sum, item_grad = dense_step(
            user_block,
            item_shard,
            ratings[tick_index],
            tile_users[tick_index],
            tile_items[tick_index],
            tile_count[tick_index, 0],
        )
        user_block = user_block * (1.0 - user_rate * shrink_rate) + user_rate * user_sum
        item_share = lax.psum_scatter(item_grad, "owner", scatter_dimension=0, tiled=True)
        item_shard = item_shard * (1.0 - item_rate * shrink_rate) + item_rate * item_share
        if tick_index + 1 < TICKS:
            item_shard = passed_along(item_shard, "band", -1)
    return (user_block.reshape(-1, R), item_shard)


def solution(mesh):
    placed = (
        P(("band", "owner"), None),
        P(("band", "owner"), None),
        P(None, ("band", "owner"), None, None),
        P(None, ("band", "owner")),
        P(None, ("band", "owner")),
        P(None, ("band", "owner")),
    )
    return jax.shard_map(
        shards,
        mesh=mesh,
        in_specs=placed,
        out_specs=(P(("band", "owner"), None), P(("band", "owner"), None)),
        check_vma=False,
    )
```

profile of v0, /device:TPU:0, one launch (start us, length us, event | category | flops | bytes accessed | tf_op | source)
XLA Modules:
  0.0 246.8 jit_solution(12641075228223250535)
XLA Ops:
  7.9 1.4 fusion.33
  10.7 0.8 slice_bitcast_fusion
  11.5 0.8 slice_bitcast_fusion.1
  12.4 2.3 fusion.32
  14.7 2.3 fusion.4
  17.0 19.1 %all-gather.4.cloned.1.call-done = f32[1024,256]{1,0:T(8,128)} async-done(((f32[128,256]{1,0:T(8,128)}), f32[1024,256]{1,0:T(8,128)}) %all-gather.4.cloned.1.call-update) | async-done | bytes 1048592 | tf_op jit(solution)/shard_map/all_gather | solution.py:40
  36.3 1.4 copy-done.2
  37.7 3.7 %bitcast_multiply_fusion.2 = f32[512,1024]{1,0:T(8,128)S(1)} fusion(f32[64,8,8,128]{3,2,1,0:T(8,128)S(1)} %bitcast.96, f32[64,8,8,128]{3,2,1,0:T(8,128)S(1)} %bitcast.95, f32[512,256]{1,0:T(8,128)S(1)} %copy-done.3, f32[1024,256]{1,0:T(8,128)} %all-gather.4.cloned.1.call-done), kind=kOutput, calls=%fused_computation.4 | convolution fusion | flops 1611661312 | bytes 7864320 | tf_op jit(solution)/shard_map/dot_general | solution.py:41
  41.4 4.4 %fusion.34 = f32[1024,256]{1,0:T(8,128)} fusion(f32[512,1024]{1,0:T(8,128)S(1)} %bitcast_multiply_fusion.2, f32[512,256]{1,0:T(8,128)S(1)} %copy-done.3), kind=kOutput, calls=%fused_computation.62 | convolution fusion | flops 1610612736 | bytes 3670016 | tf_op jit(solution)/shard_map/dot_general | solution.py:44
  45.9 36.1 %reduce-scatter.4.cloned.1.call-done = f32[128,256]{1,0:T(8,128)} async-done(((f32[1024,256]{1,0:T(8,128)}), f32[128,256]{1,0:T(8,128)}) %reduce-scatter.4.cloned.1.call-update) | async-done | bytes 131088 | tf_op jit(solution)/shard_map/reduce_scatter | solution.py:63
  82.1 0.9 multiply_add_fusion.3
  83.0 3.4 %collective-permute-start = (f32[128,256]{1,0:T(8,128)S(1)}, f32[128,256]{1,0:T(8,128)S(1)}, u32[]{:S(2)}, u32[]{:S(2)}) collective-permute-start(f32[128,256]{1,0:T(8,128)S(1)} %multiply_add_fusion.3), channel_id=1, source_target_pairs={{8,0},{16,8},{24,16},{0,24},{9,1},{17,9},{25,17},{1,25},{10,2},{18... | collective-permute-start | bytes 393224 | tf_op jit(solution)/shard_map/ppermute | solution.py:22
  86.4 2.6 %collective-permute-done = f32[128,256]{1,0:T(8,128)S(1)} collective-permute-done((f32[128,256]{1,0:T(8,128)S(1)}, f32[128,256]{1,0:T(8,128)S(1)}, u32[]{:S(2)}, u32[]{:S(2)}) %collective-permute-start) | collective-permute-done | bytes 131104 | tf_op jit(solution)/shard_map/ppermute | solution.py:22
  90.0 2.3 fusion.3
  92.4 1.8 fusion.1
  94.2 20.1 %all-gather.6.cloned.1.call-done = f32[1024,256]{1,0:T(8,128)} async-done(((f32[128,256]{1,0:T(8,128)}), f32[1024,256]{1,0:T(8,128)}) %all-gather.6.cloned.1.call-update) | async-done | bytes 1048592 | tf_op jit(solution)/shard_map/all_gather | solution.py:40
  114.5 1.4 copy-done.1
  115.9 3.7 %bitcast_multiply_fusion.1 = f32[512,1024]{1,0:T(8,128)S(1)} fusion(f32[64,8,8,128]{3,2,1,0:T(8,128)S(1)} %bitcast.97, f32[64,8,8,128]{3,2,1,0:T(8,128)S(1)} %bitcast.94, f32[512,256]{1,0:T(8,128)S(1)} %fusion.1, f32[1024,256]{1,0:T(8,128)} %all-gather.6.cloned.1.call-done), kind=kOutput, calls=%fused_computation.2 | convolution fusion | flops 1611661312 | bytes 7864320 | tf_op jit(solution)/shard_map/dot_general | solution.py:41
  119.6 4.4 %fusion.35 = f32[1024,256]{1,0:T(8,128)} fusion(f32[512,1024]{1,0:T(8,128)S(1)} %bitcast_multiply_fusion.1, f32[512,256]{1,0:T(8,128)S(1)} %fusion.1), kind=kOutput, calls=%fused_computation.63 | convolution fusion | flops 1610612736 | bytes 3670016 | tf_op jit(solution)/shard_map/dot_general | solution.py:44
  124.1 36.1 %reduce-scatter.6.cloned.1.call-done = f32[128,256]{1,0:T(8,128)} async-done(((f32[1024,256]{1,0:T(8,128)}), f32[128,256]{1,0:T(8,128)}) %reduce-scatter.6.cloned.1.call-update) | async-done | bytes 131088 | tf_op jit(solution)/shard_map/reduce_scatter | solution.py:63
  160.2 0.9 multiply_add_fusion.2
  161.2 3.4 %collective-permute-start.1 = (f32[128,256]{1,0:T(8,128)S(1)}, f32[128,256]{1,0:T(8,128)S(1)}, u32[]{:S(2)}, u32[]{:S(2)}) collective-permute-start(f32[128,256]{1,0:T(8,128)S(1)} %multiply_add_fusion.2), channel_id=1, source_target_pairs={{8,0},{16,8},{24,16},{0,24},{9,1},{17,9},{25,17},{1,25},{10,2},{18... | collective-permute-start | bytes 393224 | tf_op jit(solution)/shard_map/ppermute | solution.py:22
  164.5 2.6 %collective-permute-done.1 = f32[128,256]{1,0:T(8,128)S(1)} collective-permute-done((f32[128,256]{1,0:T(8,128)S(1)}, f32[128,256]{1,0:T(8,128)S(1)}, u32[]{:S(2)}, u32[]{:S(2)}) %collective-permute-start.1) | collective-permute-done | bytes 131104 | tf_op jit(solution)/shard_map/ppermute | solution.py:22
  169.0 2.3 fusion.2
  171.4 1.8 fusion
  173.2 19.2 %all-gather.8.cloned.1.call-done = f32[1024,256]{1,0:T(8,128)} async-done(((f32[128,256]{1,0:T(8,128)}), f32[1024,256]{1,0:T(8,128)}) %all-gather.8.cloned.1.call-update) | async-done | bytes 1048592 | tf_op jit(solution)/shard_map/all_gather | solution.py:40
  192.6 1.4 copy-done
  194.0 3.7 %bitcast_multiply_fusion = f32[512,1024]{1,0:T(8,128)S(1)} fusion(f32[64,8,8,128]{3,2,1,0:T(8,128)S(1)} %bitcast.98, f32[64,8,8,128]{3,2,1,0:T(8,128)S(1)} %bitcast.93, f32[512,256]{1,0:T(8,128)S(1)} %fusion, f32[1024,256]{1,0:T(8,128)} %all-gather.8.cloned.1.call-done), kind=kOutput, calls=%fused_computation | convolution fusion | flops 1611661312 | bytes 7864320 | tf_op jit(solution)/shard_map/dot_general | solution.py:41
  197.7 4.4 %fusion.36 = f32[1024,256]{1,0:T(8,128)} fusion(f32[512,1024]{1,0:T(8,128)S(1)} %bitcast_multiply_fusion, f32[512,256]{1,0:T(8,128)S(1)} %fusion), kind=kOutput, calls=%fused_computation.64 | convolution fusion | flops 1610612736 | bytes 3670016 | tf_op jit(solution)/shard_map/dot_general | solution.py:44
  202.2 3.9 %multiply_add_fusion = f32[512,256]{1,0:T(8,128)} fusion(f32[512,256]{1,0:T(8,128)S(1)} %fusion, f32[512,1024]{1,0:T(8,128)S(1)} %bitcast_multiply_fusion, f32[1024,256]{1,0:T(8,128)} %all-gather.8.cloned.1.call-done), kind=kOutput, calls=%fused_computation.17 | convolution fusion | flops 1611005952 | bytes 4194304 | tf_op jit(solution)/shard_map/dot_general | solution.py:43
  206.1 32.3 %reduce-scatter.8.cloned.1.call-done = f32[128,256]{1,0:T(8,128)} async-done(((f32[1024,256]{1,0:T(8,128)}), f32[128,256]{1,0:T(8,128)}) %reduce-scatter.8.cloned.1.call-update) | async-done | bytes 131088 | tf_op jit(solution)/shard_map/reduce_scatter | solution.py:63
  238.4 1.6 multiply_add_fusion.1
  (46 shorter events, 5.8 us)
Async XLA Ops:
  7.2 28.9 %all-gather.4.cloned.1.call-start = ((), (), s32[]{:S(2)}) async-start(), calls=%async_computation.3 | async-start | bytes 1179648 | tf_op jit(solution)/shard_map/all_gather | solution.py:40
  7.9 74.2 %reduce-scatter.4.cloned.1.call-start = ((), (), s32[]{:S(2)}) async-start(), calls=%async_computation.4 | async-start | bytes 1179648 | tf_op jit(solution)/shard_map/reduce_scatter | solution.py:63
  14.7 21.6 %copy-start.3 = (f32[512,256]{1,0:T(8,128)S(1)}, f32[512,256]{1,0:T(8,128)}, u32[]{:S(2)}) copy-start(f32[512,256]{1,0:T(8,128)} %param.6) | copy-start | bytes 1572868
  36.1 1.6 copy-start.2
  41.4 40.7 %copy-start.7 = (f32[128,256]{1,0:T(8,128)S(1)}, f32[128,256]{1,0:T(8,128)}, u32[]{:S(2)}) copy-start(f32[128,256]{1,0:T(8,128)} %param.7) | copy-start | bytes 393220
  45.9 68.4 %all-gather.6.cloned.1.call-start = ((), (), s32[]{:S(2)}) async-start(), calls=%async_computation.5 | async-start | bytes 1179648 | tf_op jit(solution)/shard_map/all_gather | solution.py:40
  83.0 6.0 %collective-permute-start = (f32[128,256]{1,0:T(8,128)S(1)}, f32[128,256]{1,0:T(8,128)S(1)}, u32[]{:S(2)}, u32[]{:S(2)}) collective-permute-start(f32[128,256]{1,0:T(8,128)S(1)} %multiply_add_fusion.3), channel_id=1, source_target_pairs={{8,0},{16,8},{24,16},{0,24},{9,1},{17,9},{25,17},{1,25},{10,2},{18... | collective-permute-start | bytes 393224 | tf_op jit(solution)/shard_map/ppermute | solution.py:22
  89.0 0.7 copy-start.10
  89.7 70.5 %reduce-scatter.6.cloned.1.call-start = ((), (), s32[]{:S(2)}) async-start(), calls=%async_computation.6 | async-start | bytes 1179648 | tf_op jit(solution)/shard_map/reduce_scatter | solution.py:63
  89.9 2.5 %copy-start.4 = (f32[1024,256]{1,0:T(8,128)S(1)}, f32[1024,256]{1,0:T(8,128)}, u32[]{:S(2)}) copy-start(f32[1024,256]{1,0:T(8,128)} %all-gather.4.cloned.1.call-done) | copy-start | bytes 3145732
  114.3 1.6 copy-start.1
  119.6 40.7 %copy-start.11 = (f32[128,256]{1,0:T(8,128)S(1)}, f32[128,256]{1,0:T(8,128)}, u32[]{:S(2)}) copy-start(f32[128,256]{1,0:T(8,128)} %copy-done.10) | copy-start | bytes 393220
  119.6 49.5 %copy-start.6 = (bf16[1,16,128,128]{3,2,1,0:T(8,128)(2,1)S(1)}, bf16[1,16,128,128]{3,2,1,0:T(8,128)(2,1)}, u32[]{:S(2)}) copy-start(bf16[1,16,128,128]{3,2,1,0:T(8,128)(2,1)} %get-tuple-element.2) | copy-start | bytes 1572868
  124.0 68.4 %all-gather.8.cloned.1.call-start = ((), (), s32[]{:S(2)}) async-start(), calls=%async_computation.7 | async-start | bytes 1179648 | tf_op jit(solution)/shard_map/all_gather | solution.py:40
  161.2 6.0 %collective-permute-start.1 = (f32[128,256]{1,0:T(8,128)S(1)}, f32[128,256]{1,0:T(8,128)S(1)}, u32[]{:S(2)}, u32[]{:S(2)}) collective-permute-start(f32[128,256]{1,0:T(8,128)S(1)} %multiply_add_fusion.2), channel_id=1, source_target_pairs={{8,0},{16,8},{24,16},{0,24},{9,1},{17,9},{25,17},{1,25},{10,2},{18... | collective-permute-start | bytes 393224 | tf_op jit(solution)/shard_map/ppermute | solution.py:22
  167.2 0.7 copy-start.8
  167.8 70.5 %reduce-scatter.8.cloned.1.call-start = ((), (), s32[]{:S(2)}) async-start(), calls=%async_computation.8 | async-start | bytes 1179648 | tf_op jit(solution)/shard_map/reduce_scatter | solution.py:63
  168.1 3.3 %copy-start.5 = (f32[1024,256]{1,0:T(8,128)S(1)}, f32[1024,256]{1,0:T(8,128)}, u32[]{:S(2)}) copy-start(f32[1024,256]{1,0:T(8,128)} %all-gather.6.cloned.1.call-done) | copy-start | bytes 3145732
  192.4 1.6 copy-start
  202.2 36.2 %copy-start.9 = (f32[128,256]{1,0:T(8,128)S(1)}, f32[128,256]{1,0:T(8,128)}, u32[]{:S(2)}) copy-start(f32[128,256]{1,0:T(8,128)} %copy-done.8) | copy-start | bytes 393220
Sparse Core Ops, SparseCore 0:
  9.9 26.1 all-gather.3
  46.0 36.0 reduce-scatter.3
  89.8 24.4 all-gather.5
  124.2 36.0 reduce-scatter.5
  168.0 24.4 all-gather.7
  202.3 36.0 reduce-scatter.7
where the time goes:
time: 247 us
  waiting for transfers between devices  169 us (68%)
  matrix products  39.2 us (16%)
  between operations  14.3 us (6%)
  local copies, waits for them, and re-layouts  11.4 us (5%)
  starting transfers between devices  7.4 us (3%)
  other arithmetic  5.52 us (2%)
    reduce_scatter x3, waiting for transfers between devices, shards(): lax.psum_scatter(item_grad, 'owner', scatter_dimension=0, tiled=True)  105 us
    all_gather x3, waiting for transfers between devices, dense_step(): piece = lax.all_gather(item_shard, 'owner', axis=0, tiled=True)  58.4 us
    dot_general x3, matrix products, dense_step(): item_rows = jnp.dot(errors.T, user_flat, precision=highest)  13.3 us
    dot_general x3, matrix products, dense_step(): predicted = jnp.dot(user_flat, piece.T, precision=highest)  11.1 us
    dot_general x3, matrix products, dense_step(): user_grad = jnp.dot(errors, piece, precision=highest)  7.48 us
    dot_general x3, matrix products, dense_step(): jnp.einsum('kt,ks,kui->tusi', user_hot, item_hot, rating_tiles.astype(jnp...  6.98 us
    ppermute x2, starting transfers between devices, passed_along(): return lax.ppermute(block, axis, route)  6.76 us
    unnamed x24, local copies, waits for them, and re-layouts  5.49 us
  transfers between devices with their start and end apart: 8, of which 8 were waited for; matrix products, arithmetic and copies ran while one was open for 9% of the time, Pallas kernels for 0%

commit v1 on v0

v1 whole, which is shorter than its diff:
```python
import functools

import jax
import jax.numpy as jnp
from jax import lax
from jax.experimental import pallas as pl
from jax.experimental.pallas import tpu as pltpu
from jax.sharding import PartitionSpec as P

user_rate = 0.02
item_rate = 0.005
shrink_rate = 0.05
MESH = pl.DeviceIdType.MESH
f32 = jnp.float32
bf16 = jnp.bfloat16


def halves(x):
    high = x.astype(bf16)
    return high, (x - high.astype(f32)).astype(bf16)


def dot3(a, b, dims):
    (ah, al), (bh, bl) = a, b

    def one(x, y):
        return lax.dot_general(x, y, (dims, ((), ())), preferred_element_type=f32)

    return one(ah, bh) + (one(ah, bl) + one(al, bh))


def kernel(cfg, slot_ref, live_ref, users_ref, items_ref, ratings_ref, users_out, items_out,
           panel, from_sibling, from_chips, partial, combined, grad, uh, ul, eh, el,
           fresh, ag_send, ag_recv, fwd_send, fwd_recv, ps_send, ps_recv, rs_send, rs_recv,
           pm_send, pm_recv):
    ticks, bands, chips, share, group, tile, user_tiles, item_tiles = cfg
    groups = chips // group
    wide = 2 * share * group
    band = lax.axis_index("band")
    owner = lax.axis_index("owner")
    chip, core = owner // 2, owner % 2
    mine, within = chip // group, chip % group
    sibling = (band, chip * 2 + 1 - core)

    def group_at(s):
        if groups % 2:
            return (mine + s) % groups
        return ((mine // 2 + s // 2) % (groups // 2)) * 2 + (mine % 2 + s % 2) % 2

    def chip_at(s, j):
        return group_at(s) * group + (within + j) % group

    def own(s, j):
        return s == 0 and j == 0

    def rows(c, k):
        return pl.ds(pl.multiple_of((c * 2 + k) * share, share), share)

    def within_block(s, c, k):
        return pl.ds(pl.multiple_of(((c % group) * 2 + k) * share, share), share)

    def to(c):
        return (band, c * 2 + core)

    pairs = [(s, j) for s in range(groups) for j in range(group)]
    others = [p for p in pairs if not own(*p)]
    back = ((band + bands - 1) % bands, owner)
    ahead = ((band + 1) % bands, owner)

    barrier = pltpu.get_barrier_semaphore()
    for device in [sibling, back, ahead] + [to(chip_at(*p)) for p in others]:
        pl.semaphore_signal(barrier, inc=1, device_id=device, device_id_type=MESH)
    pl.semaphore_wait(barrier, 3 + len(others))

    def remote(src, dst, ssem, rsem, device):
        return pltpu.make_async_remote_copy(
            src_ref=src, dst_ref=dst, send_sem=ssem, recv_sem=rsem,
            device_id=device, device_id_type=MESH)

    users_out[...] = users_ref[...]
    panel[0, rows(chip, core), :] = items_ref[...]

    def tick(t, carry):
        def gather(s, j):
            here = panel.at[t, rows(chip, core), :]
            c = chip_at(s, j)
            return remote(here, here, ag_send.at[t, c], ag_recv.at[t, chip], to(c))

        def gathered(s, j):
            c = chip_at(s, j)
            here = panel.at[t, rows(c, core), :]
            return remote(here, here, ag_send.at[t, c], ag_recv.at[t, c], to(c))

        def forward(s, j):
            c = chip_at(s, j)
            here = panel.at[t, rows(c, core), :]
            return remote(here, here, fwd_send.at[t, c], fwd_recv.at[t, c], sibling)

        def forwarded(s, j):
            c = chip_at(s, j)
            here = panel.at[t, rows(c, 1 - core), :]
            return remote(here, here, fwd_send.at[t, c], fwd_recv.at[t, c], sibling)

        def hand_over(s, j):
            c = chip_at(s, j)
            return remote(partial.at[s, within_block(s, c, 1 - core), :], from_sibling.at[t, c],
                          ps_send.at[t, c], ps_recv.at[t, c], sibling)

        def scatter(s, j):
            c = chip_at(s, j)
            return remote(combined.at[c], from_chips.at[t, chip],
                          rs_send.at[t, c], rs_recv.at[t, chip], to(c))

        def scattered(s, j):
            c = chip_at(s, j)
            return remote(combined.at[c], from_chips.at[t, c],
                          rs_send.at[t, c], rs_recv.at[t, c], to(c))

        def pass_back(here, there):
            return remote(fresh.at[here], panel.at[there, rows(chip, core), :],
                          pm_send.at[here], pm_recv.at[there], back)

        @pl.when(t > 0)
        def _():
            pass_back(t - 1, t).wait_recv()

        for p in others:
            gather(*p).start()
        forward(0, 0).start()

        high, low = halves(users_out[...])
        uh[...] = high
        ul[...] = low

        def block(s):
            g = group_at(s)
            v = halves(panel[t, pl.ds(pl.multiple_of(g * wide, wide), wide), :])
            for i in range(user_tiles):
                here = pl.ds(i * tile, tile)
                pred = dot3((uh[here, :], ul[here, :]), v, ((1,), (1,)))
                parts = []
                for j in range(wide // tile):
                    cell = i * item_tiles + g * (wide // tile) + j
                    rating = ratings_ref[t, slot_ref[t, cell]].astype(f32)
                    parts.append((rating - pred[:, j * tile:(j + 1) * tile]) * live_ref[t, cell])
                e = halves(jnp.concatenate(parts, axis=1))
                eh[here, :] = e[0]
                el[here, :] = e[1]
                step = dot3(e, v, ((1,), (0,)))
                if s == 0:
                    grad[here, :] = step
                else:
                    grad[here, :] += step
            partial[s] = dot3((eh[...], el[...]), (uh[...], ul[...]), ((0,), (0,)))

        def combine(s):
            for j in range(group):
                c = chip_at(s, j)
                hand_over(s, j).wait_recv()
                combined[c] = partial[s, within_block(s, c, core), :] + from_sibling[t, c]
                if not own(s, j):
                    scatter(s, j).start()

        for s in range(groups):
            for j in range(group):
                if not own(s, j):
                    gathered(s, j).wait_recv()
                    forward(s, j).start()
            if s:
                combine(s - 1)
            for j in range(group):
                forwarded(s, j).wait_recv()
            block(s)
            for j in range(group):
                hand_over(s, j).start()
        users_out[...] = users_out[...] * (1.0 - user_rate * shrink_rate) + user_rate * grad[...]
        combine(groups - 1)

        total = combined[chip]
        for p in others:
            scattered(*p).wait_recv()
            total = total + from_chips[t, chip_at(*p)]
        new = panel[t, rows(chip, core), :] * (1.0 - item_rate * shrink_rate) + item_rate * total

        @pl.when(t < ticks - 1)
        def _():
            fresh[t] = new
            pass_back(t, t + 1).start()

        @pl.when(t == ticks - 1)
        def _():
            items_out[...] = new

        for p in pairs:
            forward(*p).wait_send()
            hand_over(*p).wait_send()
            if not own(*p):
                gather(*p).wait_send()
                scatter(*p).wait_send()

        @pl.when(t > 0)
        def _():
            pass_back(t - 1, t).wait_send()

        return carry

    lax.fori_loop(0, ticks, tick, 0)


def shards(bands, owners, user_factors, item_factors, ratings, tile_users, tile_items, tile_count):
    ticks, slots, tile, _ = ratings.shape
    users, rank = user_factors.shape
    share = item_factors.shape[0]
    chips = owners // 2
    panel_rows = share * owners
    user_tiles, item_tiles = users // tile, panel_rows // tile
    group = max(1, 2 * tile // (2 * share))
    groups, wide = chips // group, 2 * share * group

    number = jnp.arange(slots, dtype=jnp.int32)[None, :]
    cell = jnp.where(number < tile_count, tile_users * item_tiles + tile_items, -1)
    hit = cell[:, :, None] == jnp.arange(user_tiles * item_tiles, dtype=jnp.int32)[None, None, :]
    slot_of = jnp.sum(jnp.where(hit, number[:, :, None], 0), axis=1)
    live = jnp.sum(hit.astype(f32), axis=1)

    cfg = (ticks, bands, chips, share, group, tile, user_tiles, item_tiles)
    vmem = pl.BlockSpec(memory_space=pltpu.VMEM)
    smem = pl.BlockSpec(memory_space=pltpu.SMEM)
    sems = pltpu.SemaphoreType.DMA((ticks, chips))
    work = 18 * ticks * users * panel_rows * rank
    return pl.pallas_call(
        functools.partial(kernel, cfg),
        out_shape=(jax.ShapeDtypeStruct((users, rank), f32), jax.ShapeDtypeStruct((share, rank), f32)),
        in_specs=[smem, smem, vmem, vmem, vmem],
        out_specs=(vmem, vmem),
        scratch_shapes=[
            pltpu.VMEM((ticks, panel_rows, rank), f32),
            pltpu.VMEM((ticks, chips, share, rank), f32),
            pltpu.VMEM((ticks, chips, share, rank), f32),
            pltpu.VMEM((groups, wide, rank), f32),
            pltpu.VMEM((chips, share, rank), f32),
            pltpu.VMEM((users, rank), f32),
            pltpu.VMEM((users, rank), bf16),
            pltpu.VMEM((users, rank), bf16),
            pltpu.VMEM((users, wide), bf16),
            pltpu.VMEM((users, wide), bf16),
            pltpu.VMEM((ticks, share, rank), f32),
        ] + [sems] * 8 + [pltpu.SemaphoreType.DMA((ticks,))] * 2,
        compiler_params=pltpu.CompilerParams(
            collective_id=0, has_side_effects=True, vmem_limit_bytes=48 * 1024 * 1024),
        cost_estimate=pl.CostEstimate(flops=work, bytes_accessed=8 * 1024 * 1024, transcendentals=0),
    )(slot_of, live, user_factors, item_factors, ratings)


def solution(mesh):
    both = ("band", "owner")
    placed = (P(both, None), P(both, None), P(None, both, None, None), P(None, both), P(None, both), P(None, both))
    return jax.shard_map(
        functools.partial(shards, mesh.shape["band"], mesh.shape["owner"]),
        mesh=mesh,
        in_specs=placed,
        out_specs=(P(both, None), P(both, None)),
        check_vma=False,
    )
```

time: 247 us -> 83.8 us (0.34)
  waiting for transfers between devices: 169 us -> 0 us
  Pallas kernels: 0 us -> 77.2 us
  matrix products: 39.2 us -> 0 us
  between operations: 14.3 us -> 0.65 us
  starting transfers between devices: 7.4 us -> 0 us
  local copies, waits for them, and re-layouts: 11.4 us -> 4.8 us
  other arithmetic: 5.52 us -> 0.95 us
    reduce_scatter x3 -> x0, waiting for transfers between devices: 105 us -> none  [shards(): lax.psum_scatter(item_grad, 'owner', scatter_dimension=0, tiled=True)]
    pallas_call x0 -> x1, Pallas kernels: none -> 77.2 us  [shards(): pl.pallas_call(functools.partial(kernel, cfg), out_shape=(jax.ShapeDtypeS...]
    all_gather x3 -> x0, waiting for transfers between devices: 58.4 us -> none  [dense_step(): piece = lax.all_gather(item_shard, 'owner', axis=0, tiled=True)]
    dot_general x15 -> x0, matrix products: 39.2 us -> none  [the longest x3 13.3 us: dense_step(): item_rows = jnp.dot(errors.T, user_flat, precision=highest)]
    ppermute x2 -> x0, starting transfers between devices: 6.76 us -> none  [passed_along(): return lax.ppermute(block, axis, route)]
    ppermute x2 -> x0, waiting for transfers between devices: 5.26 us -> none  [passed_along(): return lax.ppermute(block, axis, route)]
    slice x2 -> x0, local copies, waits for them, and re-layouts: 3.73 us -> none  [the longest x1 2.31 us: shards(): ratings[tick_index]]
    add x3 -> x0, other arithmetic: 3.43 us -> none  [shards(): item_shard * (1.0 - item_rate * shrink_rate) + item_rate * item_share]
  transfers between devices with their start and end apart: 8 -> 0, of which waited for: 8 -> 0; matrix products, arithmetic and copies ran while one was open for 9% -> 0% of each run, Pallas kernels for 0% -> 0%
where the time goes in v1:
time: 83.8 us; the launch traced here: 83.6 us
  Pallas kernels  77.2 us (92%)
  local copies, waits for them, and re-layouts  4.8 us (6%)
  other arithmetic  0.95 us (1%)
    pallas_call x1, Pallas kernels, shards(): pl.pallas_call(functools.partial(kernel, cfg), out_shape=(jax.ShapeDtypeS...  77.2 us
    unnamed x8, local copies, waits for them, and re-layouts  4.8 us

profile of v1, /device:TPU:0, one launch (start us, length us, event | category | flops | bytes accessed | tf_op | source)
XLA Modules:
  0.0 83.6 jit_solution(7148963304961842119)
XLA Ops:
  0.6 0.8 add_select_fusion
  1.4 0.1 convert_reduce_fusion.live_ref
  1.5 0.1 select_reduce_fusion.slot_ref
  1.6 0.0 copy-start
  1.6 1.4 %copy-done = bf16[3,16,128,128]{3,2,1,0:T(8,128)(2,1)S(1)} copy-done((bf16[3,16,128,128]{3,2,1,0:T(8,128)(2,1)S(1)}, bf16[3,16,128,128]{3,2,1,0:T(8,128)(2,1)}, u32[]{:S(2)}) %copy-start) | copy-done | bytes 1572888
  3.0 0.0 copy-start.1
  3.0 1.0 %copy-done.1 = f32[512,256]{1,0:T(8,128)S(1)} copy-done((f32[512,256]{1,0:T(8,128)S(1)}, f32[512,256]{1,0:T(8,128)}, u32[]{:S(2)}) %copy-start.1) | copy-done | bytes 524312
  4.0 0.0 copy-start.2
  4.0 0.9 %copy-done.2 = f32[128,256]{1,0:T(8,128)S(1)} copy-done((f32[128,256]{1,0:T(8,128)S(1)}, f32[128,256]{1,0:T(8,128)}, u32[]{:S(2)}) %copy-start.2) | copy-done | bytes 131096
  4.9 77.2 %shard_map.77 = (f32[512,256]{1,0:T(8,128)S(1)}, f32[128,256]{1,0:T(8,128)S(1)}) custom-call(s32[3,32]{1,0:T(4,128)S(1)} %select_reduce_fusion.slot_ref, f32[3,32]{1,0:T(4,128)S(1)} %convert_reduce_fusion.live_ref, f32[512,256]{1,0:T(8,128)S(1)} %copy-done.1, f32[128,256]{1,0:T(8,128)S(1)} %copy-done.2, bf16[3,16,128,128]{3,2,1,0:T(8,128)(2,1)S(1)} %copy-done), custom_call_target="tpu_custom_call" | custom-call | flops 7247757312 | bytes 8388608 | tf_op jit(solution)/shard_map/pallas_call | solution.py:231
  82.2 0.8 copy.10
  82.9 0.7 copy.11
Async XLA Ops:
  1.6 1.4 %copy-start = (bf16[3,16,128,128]{3,2,1,0:T(8,128)(2,1)S(1)}, bf16[3,16,128,128]{3,2,1,0:T(8,128)(2,1)}, u32[]{:S(2)}) copy-start(bf16[3,16,128,128]{3,2,1,0:T(8,128)(2,1)} %ratings_ref.1) | copy-start | bytes 4718596
  3.0 1.0 %copy-start.1 = (f32[512,256]{1,0:T(8,128)S(1)}, f32[512,256]{1,0:T(8,128)}, u32[]{:S(2)}) copy-start(f32[512,256]{1,0:T(8,128)} %users_ref.1) | copy-start | bytes 1572868
  4.0 0.9 %copy-start.2 = (f32[128,256]{1,0:T(8,128)S(1)}, f32[128,256]{1,0:T(8,128)}, u32[]{:S(2)}) copy-start(f32[128,256]{1,0:T(8,128)} %items_ref.1) | copy-start | bytes 393220

commit v2 on v1

--- a/solution.py
+++ b/solution.py
@@ -29,10 +29,10 @@
     return one(ah, bh) + (one(ah, bl) + one(al, bh))
 
 
-def kernel(cfg, slot_ref, live_ref, users_ref, items_ref, ratings_ref, users_out, items_out,
+def kernel(cfg, slot_ref, live_ref, users_ref, items_ref, ratings_hbm, users_out, items_out,
            panel, from_sibling, from_chips, partial, combined, grad, uh, ul, eh, el,
            fresh, ag_send, ag_recv, fwd_send, fwd_recv, ps_send, ps_recv, rs_send, rs_recv,
-           pm_send, pm_recv):
+           pm_send, pm_recv, ratings_ref, load_sem):
     ticks, bands, chips, share, group, tile, user_tiles, item_tiles = cfg
     groups = chips // group
     wide = 2 * share * group
@@ -43,6 +43,7 @@
     sibling = (band, chip * 2 + 1 - core)
 
     def group_at(s):
+        s = (groups - s) % groups
         if groups % 2:
             return (mine + s) % groups
         return ((mine // 2 + s // 2) % (groups // 2)) * 2 + (mine % 2 + s % 2) % 2
@@ -67,6 +68,11 @@
     back = ((band + bands - 1) % bands, owner)
     ahead = ((band + 1) % bands, owner)
 
+    load_users = pltpu.make_async_copy(users_ref, users_out, load_sem.at[0])
+    load_ratings = pltpu.make_async_copy(ratings_hbm, ratings_ref, load_sem.at[1])
+    load_users.start()
+    load_ratings.start()
+
     barrier = pltpu.get_barrier_semaphore()
     for device in [sibling, back, ahead] + [to(chip_at(*p)) for p in others]:
         pl.semaphore_signal(barrier, inc=1, device_id=device, device_id_type=MESH)
@@ -77,7 +83,6 @@
             src_ref=src, dst_ref=dst, send_sem=ssem, recv_sem=rsem,
             device_id=device, device_id_type=MESH)
 
-    users_out[...] = users_ref[...]
     panel[0, rows(chip, core), :] = items_ref[...]
 
     def tick(t, carry):
@@ -127,6 +132,11 @@
         for p in others:
             gather(*p).start()
         forward(0, 0).start()
+
+        @pl.when(t == 0)
+        def _():
+            load_users.wait()
+            load_ratings.wait()
 
         high, low = halves(users_out[...])
         uh[...] = high
@@ -161,11 +171,14 @@
                 if not own(s, j):
                     scatter(s, j).start()
 
-        for s in range(groups):
+        def receive(s):
             for j in range(group):
                 if not own(s, j):
                     gathered(s, j).wait_recv()
                     forward(s, j).start()
+
+        for s in range(groups):
+            receive(s)
             if s:
                 combine(s - 1)
             for j in range(group):
@@ -225,13 +238,14 @@
 
     cfg = (ticks, bands, chips, share, group, tile, user_tiles, item_tiles)
     vmem = pl.BlockSpec(memory_space=pltpu.VMEM)
+    hbm = pl.BlockSpec(memory_space=pltpu.HBM)
     smem = pl.BlockSpec(memory_space=pltpu.SMEM)
     sems = pltpu.SemaphoreType.DMA((ticks, chips))
     work = 18 * ticks * users * panel_rows * rank
     return pl.pallas_call(
         functools.partial(kernel, cfg),
         out_shape=(jax.ShapeDtypeStruct((users, rank), f32), jax.ShapeDtypeStruct((share, rank), f32)),
-        in_specs=[smem, smem, vmem, vmem, vmem],
+        in_specs=[smem, smem, hbm, vmem, hbm],
         out_specs=(vmem, vmem),
         scratch_shapes=[
             pltpu.VMEM((ticks, panel_rows, rank), f32),
@@ -245,7 +259,8 @@
             pltpu.VMEM((users, wide), bf16),
             pltpu.VMEM((users, wide), bf16),
             pltpu.VMEM((ticks, share, rank), f32),
-        ] + [sems] * 8 + [pltpu.SemaphoreType.DMA((ticks,))] * 2,
+        ] + [sems] * 8 + [pltpu.SemaphoreType.DMA((ticks,))] * 2 + [
+            pltpu.VMEM(ratings.shape, ratings.dtype), pltpu.SemaphoreType.DMA((2,))],
         compiler_params=pltpu.CompilerParams(
             collective_id=0, has_side_effects=True, vmem_limit_bytes=48 * 1024 * 1024),
         cost_estimate=pl.CostEstimate(flops=work, bytes_accessed=8 * 1024 * 1024, transcendentals=0),

time: 83.8 us -> 82.1 us (0.980)
  Pallas kernels: 77.2 us -> 74.9 us
    pallas_call x1, Pallas kernels: 77.2 us -> 74.9 us  [shards(): pl.pallas_call(functools.partial(kernel, cfg), out_shape=(jax.ShapeDtypeS...]
where the time goes in v2:
time: 82.1 us; the launch traced here: 81.3 us
  Pallas kernels  74.9 us (91%)
  local copies, waits for them, and re-layouts  4.8 us (6%)
  other arithmetic  0.95 us (1%)
    pallas_call x1, Pallas kernels, shards(): pl.pallas_call(functools.partial(kernel, cfg), out_shape=(jax.ShapeDtypeS...  74.9 us
    unnamed x8, local copies, waits for them, and re-layouts  4.8 us

profile of v2, /device:TPU:0, one launch (start us, length us, event | category | flops | bytes accessed | tf_op | source)
XLA Modules:
  0.0 81.3 jit_solution(15637810495816317573)
XLA Ops:
  0.6 0.8 add_select_fusion
  1.4 0.1 convert_reduce_fusion.live_ref
  1.5 0.1 select_reduce_fusion.slot_ref
  1.6 0.0 copy-start
  1.6 1.4 %copy-done = bf16[3,16,128,128]{3,2,1,0:T(8,128)(2,1)S(1)} copy-done((bf16[3,16,128,128]{3,2,1,0:T(8,128)(2,1)S(1)}, bf16[3,16,128,128]{3,2,1,0:T(8,128)(2,1)}, u32[]{:S(2)}) %copy-start) | copy-done | bytes 1572888
  3.0 0.0 copy-start.1
  3.0 1.0 %copy-done.1 = f32[512,256]{1,0:T(8,128)S(1)} copy-done((f32[512,256]{1,0:T(8,128)S(1)}, f32[512,256]{1,0:T(8,128)}, u32[]{:S(2)}) %copy-start.1) | copy-done | bytes 524312
  4.0 0.0 copy-start.2
  4.0 0.9 %copy-done.2 = f32[128,256]{1,0:T(8,128)S(1)} copy-done((f32[128,256]{1,0:T(8,128)S(1)}, f32[128,256]{1,0:T(8,128)}, u32[]{:S(2)}) %copy-start.2) | copy-done | bytes 131096
  4.9 74.9 %shard_map.77 = (f32[512,256]{1,0:T(8,128)S(1)}, f32[128,256]{1,0:T(8,128)S(1)}) custom-call(s32[3,32]{1,0:T(4,128)S(1)} %select_reduce_fusion.slot_ref, f32[3,32]{1,0:T(4,128)S(1)} %convert_reduce_fusion.live_ref, f32[512,256]{1,0:T(8,128)S(1)} %copy-done.1, f32[128,256]{1,0:T(8,128)S(1)} %copy-done.2, bf16[3,16,128,128]{3,2,1,0:T(8,128)(2,1)S(1)} %copy-done), custom_call_target="tpu_custom_call" | custom-call | flops 7247757312 | bytes 8388608 | tf_op jit(solution)/shard_map/pallas_call | solution.py:245
  79.8 0.8 copy.10
  80.6 0.7 copy.11
Async XLA Ops:
  1.6 1.4 %copy-start = (bf16[3,16,128,128]{3,2,1,0:T(8,128)(2,1)S(1)}, bf16[3,16,128,128]{3,2,1,0:T(8,128)(2,1)}, u32[]{:S(2)}) copy-start(bf16[3,16,128,128]{3,2,1,0:T(8,128)(2,1)} %ratings_hbm.1) | copy-start | bytes 4718596
  3.0 1.0 %copy-start.1 = (f32[512,256]{1,0:T(8,128)S(1)}, f32[512,256]{1,0:T(8,128)}, u32[]{:S(2)}) copy-start(f32[512,256]{1,0:T(8,128)} %users_ref.1) | copy-start | bytes 1572868
  4.0 0.9 %copy-start.2 = (f32[128,256]{1,0:T(8,128)S(1)}, f32[128,256]{1,0:T(8,128)}, u32[]{:S(2)}) copy-start(f32[128,256]{1,0:T(8,128)} %items_ref.1) | copy-start | bytes 393220

commit v3 on v2

--- a/solution.py
+++ b/solution.py
@@ -31,7 +31,7 @@
 
 def kernel(cfg, slot_ref, live_ref, users_ref, items_ref, ratings_hbm, users_out, items_out,
            panel, from_sibling, from_chips, partial, combined, grad, uh, ul, eh, el,
-           fresh, ag_send, ag_recv, fwd_send, fwd_recv, ps_send, ps_recv, rs_send, rs_recv,
+           vh, vl, fresh, ag_send, ag_recv, fwd_send, fwd_recv, ps_send, ps_recv, rs_send, rs_recv,
            pm_send, pm_recv, ratings_ref, load_sem):
     ticks, bands, chips, share, group, tile, user_tiles, item_tiles = cfg
     groups = chips // group
@@ -145,6 +145,8 @@
         def block(s):
             g = group_at(s)
             v = halves(panel[t, pl.ds(pl.multiple_of(g * wide, wide), wide), :])
+            vh[s] = v[0]
+            vl[s] = v[1]
             for i in range(user_tiles):
                 here = pl.ds(i * tile, tile)
                 pred = dot3((uh[here, :], ul[here, :]), v, ((1,), (1,)))
@@ -153,15 +155,29 @@
                     cell = i * item_tiles + g * (wide // tile) + j
                     rating = ratings_ref[t, slot_ref[t, cell]].astype(f32)
                     parts.append((rating - pred[:, j * tile:(j + 1) * tile]) * live_ref[t, cell])
-                e = halves(jnp.concatenate(parts, axis=1))
-                eh[here, :] = e[0]
-                el[here, :] = e[1]
-                step = dot3(e, v, ((1,), (0,)))
+                high, low = halves(jnp.concatenate(parts, axis=1))
+                eh[s, here, :] = high
+                el[s, here, :] = low
+            u = (uh[...], ul[...])
+            if group == 1 and share % tile == 0:
+                for k in (1 - core, core):
+                    part = pl.ds(pl.multiple_of(k * share, share), share)
+                    partial[s, part, :] = dot3((eh[s, :, part], el[s, :, part]), u, ((0,), (0,)))
+                    if k is not core:
+                        hand_over(s, 0).start()
+            else:
+                partial[s] = dot3((eh[s], el[s]), u, ((0,), (0,)))
+                for j in range(group):
+                    hand_over(s, j).start()
+
+        def user_step(s):
+            for i in range(user_tiles):
+                here = pl.ds(i * tile, tile)
+                step = dot3((eh[s, here, :], el[s, here, :]), (vh[s], vl[s]), ((1,), (0,)))
                 if s == 0:
                     grad[here, :] = step
                 else:
                     grad[here, :] += step
-            partial[s] = dot3((eh[...], el[...]), (uh[...], ul[...]), ((0,), (0,)))
 
         def combine(s):
             for j in range(group):
@@ -184,10 +200,10 @@
             for j in range(group):
                 forwarded(s, j).wait_recv()
             block(s)
-            for j in range(group):
-                hand_over(s, j).start()
-        users_out[...] = users_out[...] * (1.0 - user_rate * shrink_rate) + user_rate * grad[...]
         combine(groups - 1)
+        early = groups - 0
+        for s in range(early):
+            user_step(s)
 
         total = combined[chip]
         for p in others:
@@ -203,6 +219,10 @@
         @pl.when(t == ticks - 1)
         def _():
             items_out[...] = new
+
+        for s in range(early, groups):
+            user_step(s)
+        users_out[...] = users_out[...] * (1.0 - user_rate * shrink_rate) + user_rate * grad[...]
 
         for p in pairs:
             forward(*p).wait_send()
@@ -256,8 +276,10 @@
             pltpu.VMEM((users, rank), f32),
             pltpu.VMEM((users, rank), bf16),
             pltpu.VMEM((users, rank), bf16),
-            pltpu.VMEM((users, wide), bf16),
-            pltpu.VMEM((users, wide), bf16),
+            pltpu.VMEM((groups, users, wide), bf16),
+            pltpu.VMEM((groups, users, wide), bf16),
+            pltpu.VMEM((groups, wide, rank), bf16),
+            pltpu.VMEM((groups, wide, rank), bf16),
             pltpu.VMEM((ticks, share, rank), f32),
         ] + [sems] * 8 + [pltpu.SemaphoreType.DMA((ticks,))] * 2 + [
             pltpu.VMEM(ratings.shape, ratings.dtype), pltpu.SemaphoreType.DMA((2,))],

time: 82.1 us -> 73.5 us (0.90)
  Pallas kernels: 74.9 us -> 66.9 us
    pallas_call x1, Pallas kernels: 74.9 us -> 66.9 us  [shards(): pl.pallas_call(functools.partial(kernel, cfg), out_shape=(jax.ShapeDtypeS...]
where the time goes in v3:
time: 73.5 us; the launch traced here: 73.3 us
  Pallas kernels  66.9 us (91%)
  local copies, waits for them, and re-layouts  4.8 us (7%)
  other arithmetic  0.95 us (1%)
    pallas_call x1, Pallas kernels, shards(): pl.pallas_call(functools.partial(kernel, cfg), out_shape=(jax.ShapeDtypeS...  66.9 us
    unnamed x8, local copies, waits for them, and re-layouts  4.8 us

profile of v3, /device:TPU:0, one launch (start us, length us, event | category | flops | bytes accessed | tf_op | source)
XLA Modules:
  0.0 73.3 jit_solution(8644152173954300961)
XLA Ops:
  0.6 0.8 %add_select_fusion = s32[3,16]{1,0:T(4,128)S(1)} fusion(s32[3,16]{1,0:T(4,128)} %param.10, s32[3,16]{1,0:T(4,128)} %param.9, s32[3]{0:T(128)} %bitcast.1), kind=kLoop, calls=%fused_computation.3 | loop fusion | flops 192 | bytes 588 | tf_op jit(solution)/shard_map/jit(_where)/select_n | solution.py:254
  1.4 0.1 convert_reduce_fusion.live_ref
  1.5 0.1 select_reduce_fusion.slot_ref
  1.6 0.0 copy-start
  1.6 1.4 %copy-done = bf16[3,16,128,128]{3,2,1,0:T(8,128)(2,1)S(1)} copy-done((bf16[3,16,128,128]{3,2,1,0:T(8,128)(2,1)S(1)}, bf16[3,16,128,128]{3,2,1,0:T(8,128)(2,1)}, u32[]{:S(2)}) %copy-start) | copy-done | bytes 1572888
  3.0 0.0 copy-start.1
  3.0 1.0 %copy-done.1 = f32[512,256]{1,0:T(8,128)S(1)} copy-done((f32[512,256]{1,0:T(8,128)S(1)}, f32[512,256]{1,0:T(8,128)}, u32[]{:S(2)}) %copy-start.1) | copy-done | bytes 524312
  4.0 0.0 copy-start.2
  4.0 0.9 %copy-done.2 = f32[128,256]{1,0:T(8,128)S(1)} copy-done((f32[128,256]{1,0:T(8,128)S(1)}, f32[128,256]{1,0:T(8,128)}, u32[]{:S(2)}) %copy-start.2) | copy-done | bytes 131096
  4.9 66.9 %shard_map.77 = (f32[512,256]{1,0:T(8,128)S(1)}, f32[128,256]{1,0:T(8,128)S(1)}) custom-call(s32[3,32]{1,0:T(4,128)S(1)} %select_reduce_fusion.slot_ref, f32[3,32]{1,0:T(4,128)S(1)} %convert_reduce_fusion.live_ref, f32[512,256]{1,0:T(8,128)S(1)} %copy-done.1, f32[128,256]{1,0:T(8,128)S(1)} %copy-done.2, bf16[3,16,128,128]{3,2,1,0:T(8,128)(2,1)S(1)} %copy-done), custom_call_target="tpu_custom_call" | custom-call | flops 7247757312 | bytes 8388608 | tf_op jit(solution)/shard_map/pallas_call | solution.py:265
  71.8 0.8 %copy.10 = f32[512,256]{1,0:T(8,128)} copy(f32[512,256]{1,0:T(8,128)S(1)} %get-tuple-element.4) | data formatting | bytes 1048576
  72.6 0.7 copy.11
Async XLA Ops:
  1.6 1.4 %copy-start = (bf16[3,16,128,128]{3,2,1,0:T(8,128)(2,1)S(1)}, bf16[3,16,128,128]{3,2,1,0:T(8,128)(2,1)}, u32[]{:S(2)}) copy-start(bf16[3,16,128,128]{3,2,1,0:T(8,128)(2,1)} %ratings_hbm.1) | copy-start | bytes 4718596
  3.0 1.0 %copy-start.1 = (f32[512,256]{1,0:T(8,128)S(1)}, f32[512,256]{1,0:T(8,128)}, u32[]{:S(2)}) copy-start(f32[512,256]{1,0:T(8,128)} %users_ref.1) | copy-start | bytes 1572868
  4.0 0.9 %copy-start.2 = (f32[128,256]{1,0:T(8,128)S(1)}, f32[128,256]{1,0:T(8,128)}, u32[]{:S(2)}) copy-start(f32[128,256]{1,0:T(8,128)} %items_ref.1) | copy-start | bytes 393220
